TPU v7x, 256 devices: a whole 4x4x8 slice. The times are simulated.
256 devices in a mesh: leaf: 128 (over y, z_lo, x, core), band: 2 (over z_hi).
Axes of the slice: x: 4, y: 4, z: 8 (z_hi: 2, z_lo: 4; z = z_hi * 4 + z_lo), core: 2. Of those that a mesh axis runs over, the one named last changes fastest.
Arguments:
- weights: float32 [2, 1048576, 128], P('band', 'leaf'), may hold values from -6 to 6
- rates: float32 [2, 4, 2, 1048576], P('band', None, None, 'leaf'), may hold values from -16 to 16
- translate: float32 [4, 2, 64, 64], replicated, may hold values from -0.5 to 0.5
- evaluate: float32 [2, 2, 64, 64], P('band'), may hold values from -0.5 to 0.5
Outputs:
- image: float32 [1048576, 128], P(('leaf', 'band'))
All inputs are finite; a program needn't handle non-finite values.
Results may differ from a plain program's by a relative error of at most 0.0003.
Values sent between devices are 32-bit elements; how exact they have to be, the bound alone decides.
No kernel may reach another device: no remote copies, remote signals or barrier semaphores. Data moves between devices by JAX's collectives and lax.ppermute only.
A program may use at most 128 MiB of HBM per device.

v0:
```python
import jax
import jax.numpy as jnp
from jax import lax
from jax.sharding import PartitionSpec as P

HIGH = lax.Precision.HIGHEST


def from_partner(block, axis, bit):
    count = lax.axis_size(axis)
    route = []
    for low in range(count):
        high = low | 1 << bit
        if high != low and high < count:
            route += [(low, high), (high, low)]
    return lax.ppermute(block, axis, route)


def cheb_nodes(node_count):
    ticks = jnp.arange(node_count).astype(jnp.float32)
    return 0.5 * (1.0 - jnp.cos(jnp.pi * (ticks + 0.5) / node_count))


def translate_rows(rows, linear_rate, square_rate, source_nodes, matrix):
    angle = (
        linear_rate[:, :, None] * source_nodes
        + square_rate[:, :, None] * source_nodes * source_nodes
    )
    cosine = jnp.cos(angle)
    sine = jnp.sin(angle)
    real_in = rows[None, :, 0, :]
    imag_in = rows[None, :, 1, :]
    real_mod = cosine * real_in - sine * imag_in
    imag_mod = sine * real_in + cosine * imag_in
    real_out = jnp.einsum("chk,kj->chj", real_mod, matrix, precision=HIGH)
    imag_out = jnp.einsum("chk,kj->chj", imag_mod, matrix, precision=HIGH)
    return (real_out, imag_out)


def rotate_back(real_sum, imag_sum, linear_rate, square_rate, parent):
    angle = linear_rate[:, :, None] * parent + square_rate[:, :, None] * parent * parent
    cosine = jnp.cos(angle)
    sine = jnp.sin(angle)
    return jnp.stack(
        [cosine * real_sum + sine * imag_sum, cosine * imag_sum - sine * real_sum], axis=2
    )


def evaluate_rows(state, evaluate):
    eval_real = evaluate[0, 0]
    eval_imag = evaluate[0, 1]
    real_img = jnp.dot(
        state[:, 0], eval_real, precision=HIGH, preferred_element_type=jnp.float32
    ) - jnp.dot(state[:, 1], eval_imag, precision=HIGH, preferred_element_type=jnp.float32)
    imag_img = jnp.dot(
        state[:, 0], eval_imag, precision=HIGH, preferred_element_type=jnp.float32
    ) + jnp.dot(state[:, 1], eval_real, precision=HIGH, preferred_element_type=jnp.float32)
    return jnp.concatenate([real_img, imag_img], axis=1)


def per_device(weights, rates, translate, evaluate):
    box_count = weights.shape[1]
    node_count = weights.shape[2] // 2
    half_rows = box_count // 2
    level_count = translate.shape[0]
    parent = cheb_nodes(node_count)
    top = lax.axis_size("leaf").bit_length() - 1
    state = weights[0].reshape(box_count, 2, node_count)
    device = lax.axis_index("leaf")
    for level_index in range(level_count):
        bit_pos = top - 1 - level_index
        keep = device >> bit_pos & 1
        own_rates = rates[0, level_index].reshape(2, 2, half_rows)
        halves = state.reshape(2, half_rows, 2, node_count)
        kept_rows = lax.dynamic_index_in_dim(halves, keep, 0, keepdims=False)
        other_rows = lax.dynamic_index_in_dim(halves, 1 - keep, 0, keepdims=False)
        arrived = from_partner(other_rows, "leaf", bit_pos)
        lower_rows = jnp.where(keep == 0, kept_rows, arrived)
        upper_rows = jnp.where(keep == 0, arrived, kept_rows)
        real_lo, imag_lo = translate_rows(
            lower_rows, own_rates[0], own_rates[1], parent * 0.5, translate[level_index, 0]
        )
        real_hi, imag_hi = translate_rows(
            upper_rows, own_rates[0], own_rates[1], (1.0 + parent) * 0.5, translate[level_index, 1]
        )
        state = rotate_back(
            real_lo + real_hi, imag_lo + imag_hi, own_rates[0], own_rates[1], parent
        ).reshape(box_count, 2, node_count)
    partial_image = evaluate_rows(state, evaluate)
    return lax.psum_scatter(partial_image, "band", scatter_dimension=0, tiled=True)


def solution(mesh):
    in_specs = (
        P("band", "leaf", None),
        P("band", None, None, "leaf"),
        P(),
        P("band", None, None, None),
    )
    out_specs = P(("leaf", "band"), None)
    return jax.shard_map(
        per_device, mesh=mesh, in_specs=in_specs, out_specs=out_specs, check_vma=False
    )
```

profile of v0, /device:TPU:4, one launch (start us, length us, event | category | flops | bytes accessed | tf_op | source)
XLA Modules:
  0.0 609.1 jit_solution(6076389211476841965)
XLA Ops:
  6.5 5.6 copy.16
  12.2 6.6 %reshape_reshape_squeeze.3 = f32[2,4096,2,64]{1,0,3,2:T(2,128)} reshape(f32[1,8192,128]{1,2,0:T(8,128)} %copy.16) | data formatting | bytes 8388608 | tf_op jit(solution)/shard_map/reshape;reshape;squeeze | solution.py:74
  18.8 7.9 %constant_dynamic-slice_fusion.1 = (f32[1,4096,2,64]{1,0,3,2:T(1,128)S(1)}, f32[1,4096,2,64]{1,0,3,2:T(1,128)S(1)}) fusion(f32[2,4096,2,64]{1,0,3,2:T(2,128)} %reshape_reshape_squeeze.3, s32[]{:T(128)S(6)} %select_n.71, s32[]{:T(128)S(6)} %select_n.72), kind=kLoop, calls=%fused_computation.291 | loop fusion | bytes 8388616 | tf_op jit(solution)/shard_map/jit(dynamic_index_in_dim)/dynamic_slice | solution.py:75
  33.9 45.1 %collective-permute-done = f32[4096,2,64]{0,2,1:T(8,128)} collective-permute-done((f32[4096,2,64]{0,2,1:T(8,128)}, f32[4096,2,64]{0,2,1:T(8,128)}, u32[]{:S(2)}, u32[]{:S(2)}) %collective-permute-start) | collective-permute-done | bytes 2097184 | tf_op jit(solution)/shard_map/ppermute | solution.py:16
  83.4 9.9 %fusion.88 = f32[2,4096,64]{1,2,0:T(8,128)S(1)} fusion(f32[4096,64]{0,1:T(8,128)S(1)} %get-tuple-element.47, f32[4096,64]{0,1:T(8,128)S(1)} %get-tuple-element.48, f32[2,4096]{1,0:T(2,128)S(1)} %mul.861, f32[2,4096]{1,0:T(2,128)S(1)} %mul.858, f32[64]{0:T(128)S(1)} %broadcast_multiply_fusion, f32[4,2,64,64]{3,2,1,0:T(8,128)S(1)} %copy-done.3), kind=kOutput, calls=%fused_computation.118 | convolution fusion | flops 405798912 | bytes 4293120 | tf_op jit(solution)/shard_map/chk,kj->chj/dot_general | solution.py:35
  93.3 9.6 %fusion.75 = f32[2,4096,64]{1,2,0:T(8,128)S(1)} fusion(f32[4096,64]{0,1:T(8,128)S(1)} %get-tuple-element.47, f32[4096,64]{0,1:T(8,128)S(1)} %get-tuple-element.48, f32[2,4096]{1,0:T(2,128)S(1)} %mul.861, f32[2,4096]{1,0:T(2,128)S(1)} %mul.858, f32[64]{0:T(128)S(1)} %broadcast_multiply_fusion, f32[4,2,64,64]{3,2,1,0:T(8,128)S(1)} %copy-done.3), kind=kOutput, calls=%fused_computation.109 | convolution fusion | flops 405798912 | bytes 4293120 | tf_op jit(solution)/shard_map/chk,kj->chj/dot_general | solution.py:36
  102.9 10.0 %convolution_add_fusion.7 = f32[2,4096,64]{1,2,0:T(8,128)S(1)} fusion(f32[2,4096,64]{1,2,0:T(8,128)S(1)} %fusion.75, f32[4096,64]{0,1:T(8,128)S(1)} %get-tuple-element.44, f32[4096,64]{0,1:T(8,128)S(1)} %get-tuple-element.43, f32[64]{0:T(128)S(1)} %add_multiply_fusion.12, f32[2,4096]{1,0:T(2,128)S(1)} %mul.861, f32[2,4096]{1,0:T(2,128)S(1)} %mul.858, ...), kind=kOutput, calls=%fused_computation.20 | convolution fusion | flops 406323200 | bytes 6390272 | tf_op jit(solution)/shard_map/chk,kj->chj/dot_general | solution.py:36
  112.9 17.7 %subtract_bitcast_fusion.3 = (f32[2,4096,1,64]{1,3,0,2:T(8,128)S(1)}, f32[2,4096,1,64]{1,3,0,2:T(8,128)S(1)}) fusion(f32[2,4096,64]{1,2,0:T(8,128)S(1)} %convolution_add_fusion.7, f32[2,4096]{1,0:T(2,128)S(1)} %mul.861, f32[2,4096]{1,0:T(2,128)S(1)} %mul.858, f32[64]{0:T(128)S(1)} %broadcast_multiply_fusion.1, f32[2,4096,64]{1,2,0:T(8,128)S(1)} %fusion.88, ...), kind=kOutput, calls=%fused_computation.104 | convolution fusion | flops 411041792 | bytes 10650624 | tf_op jit(solution)/shard_map/chk,kj->chj/dot_general | solution.py:35
  134.5 45.2 %collective-permute-done.1 = f32[4096,2,64]{0,2,1:T(8,128)} collective-permute-done((f32[4096,2,64]{0,2,1:T(8,128)}, f32[4096,2,64]{0,2,1:T(8,128)}, u32[]{:S(2)}, u32[]{:S(2)}) %collective-permute-start.1) | collective-permute-done | bytes 2097184 | tf_op jit(solution)/shard_map/ppermute | solution.py:16
  182.4 9.6 %fusion.68 = f32[2,4096,64]{1,2,0:T(8,128)S(1)} fusion(f32[4096,64]{0,1:T(8,128)S(1)} %get-tuple-element.42, f32[4096,64]{0,1:T(8,128)S(1)} %get-tuple-element.41, f32[2,4096]{1,0:T(2,128)S(1)} %mul.851, f32[2,4096]{1,0:T(2,128)S(1)} %mul.848, f32[64]{0:T(128)S(1)} %broadcast_multiply_fusion, f32[4,2,64,64]{3,2,1,0:T(8,128)S(1)} %copy-done.3), kind=kOutput, calls=%fused_computation.100 | convolution fusion | flops 405798912 | bytes 4293120 | tf_op jit(solution)/shard_map/chk,kj->chj/dot_general | solution.py:35
  192.0 10.0 %fusion.55 = f32[2,4096,64]{1,2,0:T(8,128)S(1)} fusion(f32[4096,64]{0,1:T(8,128)S(1)} %get-tuple-element.42, f32[4096,64]{0,1:T(8,128)S(1)} %get-tuple-element.41, f32[2,4096]{1,0:T(2,128)S(1)} %mul.851, f32[2,4096]{1,0:T(2,128)S(1)} %mul.848, f32[64]{0:T(128)S(1)} %broadcast_multiply_fusion, f32[4,2,64,64]{3,2,1,0:T(8,128)S(1)} %copy-done.3), kind=kOutput, calls=%fused_computation.91 | convolution fusion | flops 405798912 | bytes 4293120 | tf_op jit(solution)/shard_map/chk,kj->chj/dot_general | solution.py:36
  202.2 9.9 %convolution_add_fusion.5 = f32[2,4096,64]{1,2,0:T(8,128)S(1)} fusion(f32[2,4096,64]{1,2,0:T(8,128)S(1)} %fusion.55, f32[4096,64]{0,1:T(8,128)S(1)} %get-tuple-element.40, f32[4096,64]{0,1:T(8,128)S(1)} %get-tuple-element.39, f32[64]{0:T(128)S(1)} %add_multiply_fusion.12, f32[2,4096]{1,0:T(2,128)S(1)} %mul.851, f32[2,4096]{1,0:T(2,128)S(1)} %mul.848, ...), kind=kOutput, calls=%fused_computation.18 | convolution fusion | flops 406323200 | bytes 6390272 | tf_op jit(solution)/shard_map/chk,kj->chj/dot_general | solution.py:36
  212.1 18.2 %subtract_bitcast_fusion.2 = (f32[2,4096,1,64]{1,3,0,2:T(8,128)S(1)}, f32[2,4096,1,64]{1,3,0,2:T(8,128)S(1)}) fusion(f32[2,4096,64]{1,2,0:T(8,128)S(1)} %convolution_add_fusion.5, f32[2,4096]{1,0:T(2,128)S(1)} %mul.851, f32[2,4096]{1,0:T(2,128)S(1)} %mul.848, f32[64]{0:T(128)S(1)} %broadcast_multiply_fusion.1, f32[2,4096,64]{1,2,0:T(8,128)S(1)} %fusion.68, ...), kind=kOutput, calls=%fused_computation.86 | convolution fusion | flops 411041792 | bytes 10650624 | tf_op jit(solution)/shard_map/chk,kj->chj/dot_general | solution.py:35
  236.0 89.0 %collective-permute-done.2 = f32[4096,2,64]{0,2,1:T(8,128)} collective-permute-done((f32[4096,2,64]{0,2,1:T(8,128)}, f32[4096,2,64]{0,2,1:T(8,128)}, u32[]{:S(2)}, u32[]{:S(2)}) %collective-permute-start.2) | collective-permute-done | bytes 2097184 | tf_op jit(solution)/shard_map/ppermute | solution.py:16
  327.8 9.6 %fusion.48 = f32[2,4096,64]{1,2,0:T(8,128)S(1)} fusion(f32[4096,64]{0,1:T(8,128)S(1)} %get-tuple-element.38, f32[4096,64]{0,1:T(8,128)S(1)} %get-tuple-element.37, f32[2,4096]{1,0:T(2,128)S(1)} %mul.841, f32[2,4096]{1,0:T(2,128)S(1)} %mul.838, f32[64]{0:T(128)S(1)} %broadcast_multiply_fusion, f32[4,2,64,64]{3,2,1,0:T(8,128)S(1)} %copy-done.3), kind=kOutput, calls=%fused_computation.82 | convolution fusion | flops 405798912 | bytes 4293120 | tf_op jit(solution)/shard_map/chk,kj->chj/dot_general | solution.py:35
  337.4 9.8 %fusion.35 = f32[2,4096,64]{1,2,0:T(8,128)S(1)} fusion(f32[4096,64]{0,1:T(8,128)S(1)} %get-tuple-element.38, f32[4096,64]{0,1:T(8,128)S(1)} %get-tuple-element.37, f32[2,4096]{1,0:T(2,128)S(1)} %mul.841, f32[2,4096]{1,0:T(2,128)S(1)} %mul.838, f32[64]{0:T(128)S(1)} %broadcast_multiply_fusion, f32[4,2,64,64]{3,2,1,0:T(8,128)S(1)} %copy-done.3), kind=kOutput, calls=%fused_computation.73 | convolution fusion | flops 405798912 | bytes 4293120 | tf_op jit(solution)/shard_map/chk,kj->chj/dot_general | solution.py:36
  347.4 9.9 %convolution_add_fusion.3 = f32[2,4096,64]{1,2,0:T(8,128)S(1)} fusion(f32[2,4096,64]{1,2,0:T(8,128)S(1)} %fusion.35, f32[4096,64]{0,1:T(8,128)S(1)} %get-tuple-element.36, f32[4096,64]{0,1:T(8,128)S(1)} %get-tuple-element.35, f32[64]{0:T(128)S(1)} %add_multiply_fusion.12, f32[2,4096]{1,0:T(2,128)S(1)} %mul.841, f32[2,4096]{1,0:T(2,128)S(1)} %mul.838, ...), kind=kOutput, calls=%fused_computation.16 | convolution fusion | flops 406323200 | bytes 6390272 | tf_op jit(solution)/shard_map/chk,kj->chj/dot_general | solution.py:36
  357.3 18.4 %subtract_bitcast_fusion.1 = (f32[2,4096,1,64]{1,3,0,2:T(8,128)S(1)}, f32[2,4096,1,64]{1,3,0,2:T(8,128)S(1)}) fusion(f32[2,4096,64]{1,2,0:T(8,128)S(1)} %convolution_add_fusion.3, f32[2,4096]{1,0:T(2,128)S(1)} %mul.841, f32[2,4096]{1,0:T(2,128)S(1)} %mul.838, f32[64]{0:T(128)S(1)} %broadcast_multiply_fusion.1, f32[2,4096,64]{1,2,0:T(8,128)S(1)} %fusion.48, ...), kind=kOutput, calls=%fused_computation.68 | convolution fusion | flops 411041792 | bytes 10650624 | tf_op jit(solution)/shard_map/chk,kj->chj/dot_general | solution.py:35
  378.6 46.1 %collective-permute-done.3 = f32[4096,2,64]{0,2,1:T(8,128)} collective-permute-done((f32[4096,2,64]{0,2,1:T(8,128)}, f32[4096,2,64]{0,2,1:T(8,128)}, u32[]{:S(2)}, u32[]{:S(2)}) %collective-permute-start.3) | collective-permute-done | bytes 2097184 | tf_op jit(solution)/shard_map/ppermute | solution.py:16
  427.4 9.6 %fusion.28 = f32[2,4096,64]{1,2,0:T(8,128)S(1)} fusion(f32[4096,64]{0,1:T(8,128)S(1)} %get-tuple-element.34, f32[4096,64]{0,1:T(8,128)S(1)} %get-tuple-element.33, f32[64]{0:T(128)S(1)} %broadcast_multiply_fusion, f32[2,4096]{1,0:T(2,128)S(1)} %mul.828, f32[2,4096]{1,0:T(2,128)S(1)} %mul.823, f32[4,2,64,64]{3,2,1,0:T(8,128)S(1)} %copy-done.3), kind=kOutput, calls=%fused_computation.64 | convolution fusion | flops 405798912 | bytes 4293120 | tf_op jit(solution)/shard_map/chk,kj->chj/dot_general | solution.py:35
  437.1 9.8 %fusion.15 = f32[2,4096,64]{1,2,0:T(8,128)S(1)} fusion(f32[4096,64]{0,1:T(8,128)S(1)} %get-tuple-element.34, f32[4096,64]{0,1:T(8,128)S(1)} %get-tuple-element.33, f32[64]{0:T(128)S(1)} %broadcast_multiply_fusion, f32[2,4096]{1,0:T(2,128)S(1)} %mul.828, f32[2,4096]{1,0:T(2,128)S(1)} %mul.823, f32[4,2,64,64]{3,2,1,0:T(8,128)S(1)} %copy-done.3), kind=kOutput, calls=%fused_computation.55 | convolution fusion | flops 405798912 | bytes 4293120 | tf_op jit(solution)/shard_map/chk,kj->chj/dot_general | solution.py:36
  447.1 10.1 %convolution_add_fusion.1 = f32[2,4096,64]{1,2,0:T(8,128)S(1)} fusion(f32[2,4096,64]{1,2,0:T(8,128)S(1)} %fusion.15, f32[4096,64]{0,1:T(8,128)S(1)} %get-tuple-element.32, f32[4096,64]{0,1:T(8,128)S(1)} %get-tuple-element.31, f32[64]{0:T(128)S(1)} %add_multiply_fusion.12, f32[2,4096]{1,0:T(2,128)S(1)} %mul.828, f32[2,4096]{1,0:T(2,128)S(1)} %mul.823, ...), kind=kOutput, calls=%fused_computation.14 | convolution fusion | flops 406323200 | bytes 6390272 | tf_op jit(solution)/shard_map/chk,kj->chj/dot_general | solution.py:36
  457.2 18.0 %subtract_bitcast_fusion = (f32[2,8,8,4096]{3,2,1,0:T(8,128)S(1)}, f32[2,8,8,4096]{3,2,1,0:T(8,128)S(1)}) fusion(f32[2,4096,64]{1,2,0:T(8,128)S(1)} %convolution_add_fusion.1, f32[2,4096]{1,0:T(2,128)S(1)} %mul.828, f32[64]{0:T(128)S(1)} %broadcast_multiply_fusion.1, f32[2,4096]{1,0:T(2,128)S(1)} %mul.823, f32[2,4096,64]{1,2,0:T(8,128)S(1)} %fusion.28, ...), kind=kOutput, calls=%fused_computation.50 | convolution fusion | flops 411041792 | bytes 10650624 | tf_op jit(solution)/shard_map/chk,kj->chj/dot_general | solution.py:35
  486.7 112.5 %reduce-scatter.2.cloned.1.call-done = f32[4096,128]{0,1:T(8,128)} async-done(((f32[8192,128]{0,1:T(8,128)}), f32[4096,128]{0,1:T(8,128)}) %reduce-scatter.2.cloned.1.call-update) | async-done | bytes 2097168 | tf_op jit(solution)/shard_map/reduce_scatter | solution.py:90
  (53 shorter events, 46.6 us)
Async XLA Ops:
  6.5 592.7 %reduce-scatter.2.cloned.1.call-start = ((), (), s32[]{:S(2)}) async-start(), calls=%async_computation.1 | async-start | bytes 6291456 | tf_op jit(solution)/shard_map/reduce_scatter | solution.py:90
  26.7 6.3 %copy-start.5 = (f32[1,4,2,8192]{3,2,1,0:T(2,128)S(1)}, f32[1,4,2,8192]{3,2,1,0:T(2,128)}, u32[]{:S(2)}) copy-start(f32[1,4,2,8192]{3,2,1,0:T(2,128)} %param.5) | copy-start | bytes 786436
  29.7 49.3 %collective-permute-start = (f32[4096,2,64]{0,2,1:T(8,128)}, f32[4096,2,64]{0,2,1:T(8,128)}, u32[]{:S(2)}, u32[]{:S(2)}) collective-permute-start(f32[4096,2,64]{0,2,1:T(8,128)} %bitcast.175), channel_id=1, source_target_pairs={{0,128},{128,0},{2,130},{130,2},{4,132},{132,4},{6,134},{134,6},{8... | collective-permute-start | bytes 6291464 | tf_op jit(solution)/shard_map/ppermute | solution.py:16
  82.4 1.0 copy-start.3
  130.7 2.0 copy-start.1
  132.6 47.0 %collective-permute-start.1 = (f32[4096,2,64]{0,2,1:T(8,128)}, f32[4096,2,64]{0,2,1:T(8,128)}, u32[]{:S(2)}, u32[]{:S(2)}) collective-permute-start(f32[4096,2,64]{0,2,1:T(8,128)} %fusion.9), channel_id=1, source_target_pairs={{0,64},{64,0},{2,66},{66,2},{4,68},{68,4},{6,70},{70,6},{8,72},{72... | collective-permute-start | bytes 6291464 | tf_op jit(solution)/shard_map/ppermute | solution.py:16
  230.3 2.0 copy-start
  232.3 92.7 %collective-permute-start.2 = (f32[4096,2,64]{0,2,1:T(8,128)}, f32[4096,2,64]{0,2,1:T(8,128)}, u32[]{:S(2)}, u32[]{:S(2)}) collective-permute-start(f32[4096,2,64]{0,2,1:T(8,128)} %fusion.5), channel_id=1, source_target_pairs={{0,32},{32,0},{2,34},{34,2},{4,36},{36,4},{6,38},{38,6},{8,40},{40... | collective-permute-start | bytes 6291464 | tf_op jit(solution)/shard_map/ppermute | solution.py:16
  375.7 2.0 copy-start.2
  377.7 47.0 %collective-permute-start.3 = (f32[4096,2,64]{0,2,1:T(8,128)}, f32[4096,2,64]{0,2,1:T(8,128)}, u32[]{:S(2)}, u32[]{:S(2)}) collective-permute-start(f32[4096,2,64]{0,2,1:T(8,128)} %fusion.1), channel_id=1, source_target_pairs={{0,16},{16,0},{2,18},{18,2},{4,20},{20,4},{6,22},{22,6},{8,24},{24... | collective-permute-start | bytes 6291464 | tf_op jit(solution)/shard_map/ppermute | solution.py:16
  475.2 0.8 copy-start.4
Sparse Core Ops, SparseCore 0:
  486.8 112.3 reduce-scatter.1
where the time goes:
time: 616 us; the launch traced here: 609 us
  waiting for transfers between devices  338 us (55%)
  matrix products  198 us (32%)
  local copies, waits for them, and re-layouts  30.5 us (5%)
  other arithmetic  18.6 us (3%)
  between operations  14 us (2%)
  starting transfers between devices  9.63 us (2%)
    ppermute x4, waiting for transfers between devices, from_partner(): return lax.ppermute(block, axis, route)  225 us
    reduce_scatter x1, waiting for transfers between devices, per_device(): lax.psum_scatter(partial_image, 'band', scatter_dimension=0, tiled=True)  113 us
    dot_general x8, matrix products, translate_rows(): real_out = jnp.einsum('chk,kj->chj', real_mod, matrix, precision=HIGH)  111 us
    dot_general x8, matrix products, translate_rows(): imag_out = jnp.einsum('chk,kj->chj', imag_mod, matrix, precision=HIGH)  79.2 us
  transfers between devices with their start and end apart: 5, of which 5 were waited for; matrix products, arithmetic and copies ran while one was open for 0% of the time, Pallas kernels for 0%

commit v1 on v0

v1 whole, which is shorter than its diff:
```python
import functools

import jax
import jax.numpy as jnp
import ml_dtypes
import numpy as np
from jax import lax
from jax.experimental import pallas as pl
from jax.experimental.pallas import tpu as pltpu
from jax.sharding import Mesh, PartitionSpec as P

BF = jnp.bfloat16
F32 = jnp.float32
LANES = 128
GROUP = 32
TILE = 16
MAGIC = 12582912.0


def split3(values):
    parts = []
    rest = values.astype(np.float64)
    for _ in range(3):
        part = rest.astype(ml_dtypes.bfloat16).astype(np.float64)
        parts.append(part)
        rest = rest - part
    return parts


def angle_rows(linear, square, offset):
    l1, l2, l3 = split3(linear)
    s1, s2, s3 = split3(square)
    zero = np.zeros_like(linear)
    return [l1, s1, l2, s2, l3, s3, l1, s1, l2, s2, l1, s1, offset, zero, zero, zero]


def angle_matrix(node_count):
    ticks = np.arange(node_count, dtype=np.float64)
    nodes = 0.5 * (1.0 - np.cos(np.pi * (ticks + 0.5) / node_count))
    both = np.concatenate([nodes, nodes])
    turn = 1.0 / (2.0 * np.pi)
    quarter = np.concatenate([np.zeros(node_count), np.full(node_count, -0.25)])
    zero = np.zeros(2 * node_count)
    low, high = both / 2, (1 + both) / 2
    own = np.concatenate(
        [
            np.stack(angle_rows(low * turn, low**2 * turn, quarter)),
            np.stack(angle_rows(high * turn, high**2 * turn, quarter)),
        ],
        axis=1,
    )
    undo = np.stack(angle_rows(-both * turn, -(both**2) * turn, zero))
    undo_quarter = np.stack(angle_rows(-both * turn, -(both**2) * turn, quarter))
    none = np.zeros_like(undo)
    level = np.concatenate(
        [own, np.concatenate([undo, none], 1), np.concatenate([none, undo], 1)], 0
    )
    last = np.concatenate(
        [np.concatenate([undo_quarter, none], 1), np.concatenate([none, undo_quarter], 1)], 0
    )
    return np.concatenate([level, last], 0).astype(ml_dtypes.bfloat16)


def cos_turns(t):
    r = t - ((t + MAGIC) - MAGIC)
    w = 0.25 - jnp.abs(r)
    z = w * w
    p = z * C4 + C3
    p = p * z + C2
    p = p * z + C1
    p = p * z + C0
    return p * w


def _fit():
    w = np.cos(np.pi * (np.arange(400) + 0.5) / 800) * 0.25
    z = w * w
    target = np.sin(2 * np.pi * w) / w
    basis = np.stack([z**n for n in range(5)], 1)
    return [float(c) for c in np.linalg.lstsq(basis * w[:, None], target * w, rcond=None)[0]]


C0, C1, C2, C3, C4 = _fit()


def kernel(rows, got_ref, mats_ref, angle_ref, out_ref, tiles, state_a, state_b):
    levels = 4
    row_id = lax.broadcasted_iota(jnp.int32, (TILE, rows), 0)
    even = row_id % 2 == 0

    def make_tiles(m, carry):
        for level in range(levels):
            for child in range(2):
                at = 2 * rows + level * 4 + child
                a = got_ref[m, at : at + 1, :]
                q = got_ref[m, at + 2 : at + 3, :]
                base = jnp.where(even, jnp.broadcast_to(a, even.shape), jnp.broadcast_to(q, even.shape))
                first = base.astype(BF).astype(F32)
                rest = base - first
                second = rest.astype(BF).astype(F32)
                third = rest - second
                tile = jnp.where(row_id < 6, first, jnp.where(row_id < 10, second, third))
                tile = jnp.where(row_id < 12, tile, jnp.where(row_id == 12, 1.0, 0.0))
                tiles[level, m, child] = tile.astype(BF)
        return carry

    lax.fori_loop(0, GROUP, make_tiles, 0)

    def angles(parts, matrix):
        return lax.dot_general(
            jnp.concatenate(parts, 0) if len(parts) > 1 else parts[0],
            matrix,
            (((0,), (0,)), ((), ())),
            preferred_element_type=F32,
        )

    def combine(sources, turns, stage):
        highs, lows = [], []
        for pairs, turn in zip(sources, turns):
            phase = cos_turns(turn)
            high, low = [], []
            for s in range(2):
                cs = phase[:, s * LANES : (s + 1) * LANES]
                for value in pairs[s]:
                    product = value * cs
                    top = product.astype(BF)
                    high.append(top)
                    low.append((product - top.astype(F32)).astype(BF))
            highs.append(jnp.concatenate(high, 1))
            lows.append(jnp.concatenate(low, 1))
        wide = jnp.dot(jnp.concatenate(highs, 0), mats_ref[stage], preferred_element_type=F32)
        narrow = jnp.dot(
            jnp.concatenate(lows, 0), mats_ref[stage, :, :LANES], preferred_element_type=F32
        )
        return wide[:, :LANES] + wide[:, LANES:] + narrow

    def swap(x):
        return pltpu.roll(x, LANES // 2, 1)

    def level_stage(level, read, write):
        bit = levels - 1 - level

        def body(m, carry):
            e = (m >> (bit + 1)) & 1
            k1 = m | (2 << bit)
            k0 = k1 - (2 << bit)
            x0, x1 = read(k0, e), read(k1, e)
            pairs = ((x0, swap(x0)), (x1, swap(x1)))
            turns = []
            for child in range(2):
                parts = [tiles[level, m, child]]
                if level:
                    parts += [tiles[level - 1, k0, e], tiles[level - 1, k1, e]]
                turns.append(angles(parts, angle_ref[: TILE * len(parts), :]))
            u = combine([pairs, pairs], turns, level)
            write[m, 0] = u[:rows]
            write[m, 1] = u[rows:]
            return carry

        lax.fori_loop(0, GROUP, body, 0, unroll=4)

    def read_got(k, e):
        return got_ref[k, pl.ds(pl.multiple_of(e * rows, rows), rows), :]

    level_stage(0, read_got, state_a)
    level_stage(1, lambda k, e: state_a[k, e], state_b)
    level_stage(2, lambda k, e: state_b[k, e], state_a)
    level_stage(3, lambda k, e: state_a[k, e], state_b)

    def last(i, carry):
        sources, turns = [], []
        for child in range(2):
            x0, x1 = state_b[2 * i, child], state_b[2 * i + 1, child]
            sources.append(((x0, swap(x0)), (x1, swap(x1))))
            parts = [tiles[levels - 1, 2 * i, child], tiles[levels - 1, 2 * i + 1, child]]
            turns.append(angles(parts, angle_ref[3 * TILE : 5 * TILE, :]))
        u = combine(sources, turns, levels)
        out_ref[2 * i] = u[:rows]
        out_ref[2 * i + 1] = u[rows:]
        return carry

    lax.fori_loop(0, GROUP // 2, last, 0, unroll=4)


def butterfly(got, mats, angle, rows):
    return pl.pallas_call(
        functools.partial(kernel, rows),
        out_shape=jax.ShapeDtypeStruct((GROUP, rows, LANES), F32),
        in_specs=[pl.BlockSpec(memory_space=pltpu.VMEM)] * 3,
        out_specs=pl.BlockSpec(memory_space=pltpu.VMEM),
        scratch_shapes=[
            pltpu.VMEM((4, GROUP, 2, TILE, rows), BF),
            pltpu.VMEM((GROUP, 2, rows, LANES), F32),
            pltpu.VMEM((GROUP, 2, rows, LANES), F32),
        ],
        compiler_params=pltpu.CompilerParams(vmem_limit_bytes=40 << 20),
    )(got, mats, angle)


def stage_matrices(translate, evaluate):
    zero = jnp.zeros_like(translate)
    levels = jnp.concatenate(
        [
            jnp.concatenate([translate, zero], -1),
            jnp.concatenate([-translate, zero], -1),
            jnp.concatenate([zero, translate], -1),
            jnp.concatenate([zero, translate], -1),
        ],
        axis=2,
    ).reshape(translate.shape[0], -1, LANES)
    er, ei = evaluate[:, 0], evaluate[:, 1]
    direct = jnp.concatenate([er, ei], -1)
    cross = jnp.concatenate([-ei, er], -1)
    last = jnp.concatenate([direct, -direct, cross, cross], axis=1).reshape(1, -1, LANES)
    whole = jnp.concatenate([levels, last], 0)
    high = lax.reduce_precision(whole, 8, 7)
    return jnp.concatenate([high, whole - high], -1).astype(BF)


def per_device(weights, rates, translate, evaluate):
    half = weights.shape[1] // 2
    rows = half // GROUP
    axes = ("y", "zl", "band")
    other = lax.ppermute(evaluate[0], "band", [(0, 1), (1, 0)])
    mine = lax.axis_index("band")
    both = jnp.stack(
        [jnp.where(mine == 0, evaluate[0], other), jnp.where(mine == 0, other, evaluate[0])]
    )
    mats = stage_matrices(translate, both)
    halves = weights[0].reshape(2, GROUP, rows, LANES)
    phase_rates = rates[0].reshape(16, GROUP, rows).transpose(1, 0, 2)
    message = jnp.concatenate([halves[0], halves[1], phase_rates], axis=1)
    got = lax.all_to_all(message, axes, 0, 0, tiled=True)
    angle = jnp.asarray(angle_matrix(LANES // 2))
    image = butterfly(got, mats, angle, rows)
    return lax.all_to_all(image, axes, 0, 0, tiled=True).reshape(half, LANES)


def solution(mesh):
    fine = Mesh(mesh.devices.reshape(4, 4, 4, 2, 2), ("y", "zl", "x", "core", "band"))
    leaf = ("y", "zl", "x", "core")
    return jax.shard_map(
        per_device,
        mesh=fine,
        in_specs=(P("band", leaf, None), P("band", None, None, leaf), P(), P("band", None, None, None)),
        out_specs=P((*leaf, "band"), None),
        check_vma=False,
    )
```

time: 616 us -> 249 us (0.40); the launches traced: 609 us -> 249 us
  waiting for transfers between devices: 338 us -> 99.7 us
  matrix products: 198 us -> 0 us
  Pallas kernels: 0 us -> 65.2 us
  blocking collectives: 0 us -> 57.9 us
  local copies, waits for them, and re-layouts: 30.5 us -> 5.29 us
  other arithmetic: 18.6 us -> 3.18 us
  between operations: 14 us -> 0.12 us
  starting transfers between devices: 9.63 us -> 17.4 us
    dot_general x20 -> x0, matrix products: 198 us -> none  [the longest x8 111 us: translate_rows(): real_out = jnp.einsum('chk,kj->chj', real_mod, matrix, precision=HIGH)]
    ppermute x4 -> x1, waiting for transfers between devices: 225 us -> 98 us  [per_device(): other = lax.ppermute(evaluate[0], 'band', [(0, 1), (1, 0)])]
    reduce_scatter x1 -> x0, waiting for transfers between devices: 113 us -> none  [per_device(): lax.psum_scatter(partial_image, 'band', scatter_dimension=0, tiled=True)]
    pallas_call x0 -> x1, Pallas kernels: none -> 65.2 us  [butterfly(): pl.pallas_call(functools.partial(kernel, rows), out_shape=jax.ShapeDtypeS...]
    all_to_all x0 -> x1, blocking collectives: none -> 57.9 us  [per_device(): return lax.all_to_all(image, axes, 0, 0, tiled=True).reshape(half, LANES)]
    all_to_all x0 -> x1, starting transfers between devices: none -> 11.7 us  [per_device(): got = lax.all_to_all(message, axes, 0, 0, tiled=True)]
    select_n x4 -> x0, other arithmetic: 11.1 us -> none  [per_device(): upper_rows = jnp.where(keep == 0, arrived, kept_rows)]
    unnamed x14 -> x7, local copies, waits for them, and re-layouts: 10.6 us -> 1.33 us
  transfers between devices with their start and end apart: 5 -> 2, of which waited for: 5 -> 2; matrix products, arithmetic and copies ran while one was open for 0% -> 0% of each run, Pallas kernels for 0% -> 0%
where the time goes in v1:
time: 249 us
  waiting for transfers between devices  99.7 us (40%)
  Pallas kernels  65.2 us (26%)
  blocking collectives  57.9 us (23%)
  starting transfers between devices  17.4 us (7%)
  local copies, waits for them, and re-layouts  5.29 us (2%)
  other arithmetic  3.18 us (1%)
    ppermute x1, waiting for transfers between devices, per_device(): other = lax.ppermute(evaluate[0], 'band', [(0, 1), (1, 0)])  98 us
    pallas_call x1, Pallas kernels, butterfly(): pl.pallas_call(functools.partial(kernel, rows), out_shape=jax.ShapeDtypeS...  65.2 us
    all_to_all x1, blocking collectives, per_device(): return lax.all_to_all(image, axes, 0, 0, tiled=True).reshape(half, LANES)  57.9 us
    all_to_all x1, starting transfers between devices, per_device(): got = lax.all_to_all(message, axes, 0, 0, tiled=True)  11.7 us
    ppermute x1, starting transfers between devices, per_device(): other = lax.ppermute(evaluate[0], 'band', [(0, 1), (1, 0)])  5.72 us
  transfers between devices with their start and end apart: 2, of which 2 were waited for; matrix products, arithmetic and copies ran while one was open for 0% of the time, Pallas kernels for 0%

profile of v1, /device:TPU:4, one launch (start us, length us, event | category | flops | bytes accessed | tf_op | source)
XLA Modules:
  0.0 248.9 jit_solution(18278719815320652835)
XLA Ops:
  0.0 1.2 reshape_squeeze.4
  1.2 0.2 copy.11
  1.3 2.5 %fusion.9 = (f32[1,4096,128]{2,1,0:T(8,128)S(1)}, f32[1,4096,128]{2,1,0:T(8,128)S(1)}) fusion(f32[1,8192,128]{2,1,0:T(8,128)} %param.5), kind=kLoop, calls=%fused_computation.25 | loop fusion | bytes 8388608 | tf_op jit(solution)/shard_map/slice | solution.py:232
  3.8 2.4 pad_maximum_fusion
  6.3 0.0 copy-start.2
  6.3 0.0 copy-start.1
  6.3 11.7 %all-to-all-start = ((f32[32,272,128]{2,1,0:T(8,128)}), f32[32,272,128]{2,1,0:T(8,128)}, u32[]{:S(2)}, u32[]{:S(2)}) async-start(f32[32,272,128]{2,1,0:T(8,128)} %pad_maximum_fusion), calls=%async_computation | async-start | bytes 8912896 | tf_op jit(solution)/shard_map/all_to_all | solution.py:233
  18.0 0.0 copy-done.2
  18.0 5.7 %collective-permute-start = (f32[2,64,64]{2,1,0:T(8,128)S(1)}, f32[2,64,64]{2,1,0:T(8,128)S(1)}, u32[]{:S(2)}, u32[]{:S(2)}) collective-permute-start(f32[2,64,64]{2,1,0:T(8,128)S(1)} %bitcast.28), channel_id=1, source_target_pairs={{0,1},{1,0},{2,3},{3,2},{4,5},{5,4},{6,7},{7,6},{8,9},{9,8},{10,11... | collective-permute-start | bytes 98312 | tf_op jit(solution)/shard_map/ppermute | solution.py:224
  23.8 0.0 copy-done.1
  23.8 0.1 concatenate.35
  23.9 0.1 fusion.2
  24.0 98.0 %collective-permute-done = f32[2,64,64]{2,1,0:T(8,128)S(1)} collective-permute-done((f32[2,64,64]{2,1,0:T(8,128)S(1)}, f32[2,64,64]{2,1,0:T(8,128)S(1)}, u32[]{:S(2)}, u32[]{:S(2)}) %collective-permute-start) | collective-permute-done | bytes 32800 | tf_op jit(solution)/shard_map/ppermute | solution.py:224
  122.1 0.1 maximum_negate_fusion
  122.2 0.1 maximum_maximum_fusion
  122.3 0.0 copy-start
  122.3 0.2 reduce-precision_convert_fusion
  122.6 0.1 pad_maximum_fusion.2.mats_ref
  122.8 1.7 all-to-all-done.got_ref
  124.4 0.0 copy-done
  124.4 65.2 %shard_map.55 = f32[32,128,128]{2,1,0:T(8,128)S(1)} custom-call(f32[32,272,128]{2,1,0:T(8,128)} %all-to-all-done.got_ref, bf16[5,512,256]{2,1,0:T(8,128)(2,1)S(1)} %pad_maximum_fusion.2.mats_ref, bf16[80,256]{1,0:T(8,128)(2,1)S(1)} %copy-done), custom_call_target="tpu_custom_call" | custom-call | tf_op jit(solution)/shard_map/pallas_call | solution.py:186
  189.6 57.9 %all_to_all.10 = f32[32,128,128]{2,1,0:T(8,128)S(1)} all-to-all(f32[32,128,128]{2,1,0:T(8,128)S(1)} %shard_map.55), channel_id=1, replica_groups=mesh['y'=4,'zl'=4,'x'=4,'core'=2,'band'=2] {'y','zl','band'}, dimensions={0} | all-to-all | bytes 4194304 | tf_op jit(solution)/shard_map/all_to_all | solution.py:236
  247.6 1.3 copy.13
  (4 shorter events, 0.1 us)
Async XLA Ops:
  6.3 11.7 %copy-start.2 = (f32[1,2,64,64]{3,2,1,0:T(8,128)S(1)}, f32[1,2,64,64]{3,2,1,0:T(8,128)}, u32[]{:S(2)}) copy-start(f32[1,2,64,64]{3,2,1,0:T(8,128)} %param.8) | copy-start | bytes 98308
  6.3 17.5 %copy-start.1 = (f32[4,2,64,64]{3,2,1,0:T(8,128)S(1)}, f32[4,2,64,64]{3,2,1,0:T(8,128)}, u32[]{:S(2)}) copy-start(f32[4,2,64,64]{3,2,1,0:T(8,128)} %param.7) | copy-start | bytes 393220
  6.3 118.1 %all-to-all-start = ((f32[32,272,128]{2,1,0:T(8,128)}), f32[32,272,128]{2,1,0:T(8,128)}, u32[]{:S(2)}, u32[]{:S(2)}) async-start(f32[32,272,128]{2,1,0:T(8,128)} %pad_maximum_fusion), calls=%async_computation | async-start | bytes 8912896 | tf_op jit(solution)/shard_map/all_to_all | solution.py:233
  18.0 104.0 %collective-permute-start = (f32[2,64,64]{2,1,0:T(8,128)S(1)}, f32[2,64,64]{2,1,0:T(8,128)S(1)}, u32[]{:S(2)}, u32[]{:S(2)}) collective-permute-start(f32[2,64,64]{2,1,0:T(8,128)S(1)} %bitcast.28), channel_id=1, source_target_pairs={{0,1},{1,0},{2,3},{3,2},{4,5},{5,4},{6,7},{7,6},{8,9},{9,8},{10,11... | collective-permute-start | bytes 98312 | tf_op jit(solution)/shard_map/ppermute | solution.py:224
  122.3 2.1 copy-start

commit v2 on v1

v2 whole, which is shorter than its diff:
```python
import functools

import jax
import jax.numpy as jnp
import ml_dtypes
import numpy as np
from jax import lax
from jax.experimental import pallas as pl
from jax.experimental.pallas import tpu as pltpu
from jax.sharding import Mesh, PartitionSpec as P

BF = jnp.bfloat16
F32 = jnp.float32
LANES = 128
GROUP = 32
TILE = 16
MAGIC = 12582912.0
LEVELS = 4
HALF = 64
SLICE = 128
FIRST = 96
STEPS = (4, 16)
UNROLL = 2


def split3(values):
    parts = []
    rest = values.astype(np.float64)
    for _ in range(3):
        part = rest.astype(ml_dtypes.bfloat16).astype(np.float64)
        parts.append(part)
        rest = rest - part
    return parts


def angle_rows(linear, square, offset):
    l1, l2, l3 = split3(linear)
    s1, s2, s3 = split3(square)
    zero = np.zeros_like(linear)
    return [l1, s1, l2, s2, l3, s3, l1, s1, l2, s2, l1, s1, offset, zero, zero, zero]


def angle_matrix(node_count):
    ticks = np.arange(node_count, dtype=np.float64)
    nodes = 0.5 * (1.0 - np.cos(np.pi * (ticks + 0.5) / node_count))
    both = np.concatenate([nodes, nodes])
    turn = 1.0 / (2.0 * np.pi)
    quarter = np.concatenate([np.zeros(node_count), np.full(node_count, -0.25)])
    zero = np.zeros(2 * node_count)
    low, high = both / 2, (1 + both) / 2
    own = np.concatenate(
        [
            np.stack(angle_rows(low * turn, low**2 * turn, quarter)),
            np.stack(angle_rows(high * turn, high**2 * turn, quarter)),
        ],
        axis=1,
    )
    undo = np.stack(angle_rows(-both * turn, -(both**2) * turn, zero))
    undo_quarter = np.stack(angle_rows(-both * turn, -(both**2) * turn, quarter))
    wide = 2 * node_count
    out = np.zeros((LEVELS + 1, 2 * LANES, 2 * wide))
    for level in range(LEVELS):
        out[level, TILE * level : TILE * (level + 1)] = own
        if level:
            at = HALF + TILE * (level - 1)
            out[level, at : at + TILE, :wide] = undo
            at = LANES + TILE * (level - 1)
            out[level, at : at + TILE, wide:] = undo
    at = TILE * (LEVELS - 1)
    out[LEVELS, at : at + TILE, :wide] = undo_quarter
    out[LEVELS, HALF + at : HALF + at + TILE, wide:] = undo_quarter
    return out.astype(ml_dtypes.bfloat16)


def cos_turns(t):
    r = t - ((t + MAGIC) - MAGIC)
    w = 0.25 - jnp.abs(r)
    z = w * w
    p = z * C3 + C2
    p = p * z + C1
    p = p * z + C0
    return p * w


def _fit():
    w = np.cos(np.pi * (np.arange(400) + 0.5) / 800) * 0.25
    z = w * w
    target = np.sin(2 * np.pi * w) / w
    basis = np.stack([z**n for n in range(4)], 1)
    return [float(c) for c in np.linalg.lstsq(basis * w[:, None], target * w, rcond=None)[0]]


C0, C1, C2, C3 = _fit()


def kernel(rows, lane, step, got_ref, rates_ref, mats_ref, angle_ref, out_ref, turns_ref, state_a, state_b):
    levels = LEVELS
    wide_rows = 2 * rows
    row_id = lax.broadcasted_iota(jnp.int32, (TILE, wide_rows), 0)
    even = row_id % 2 == 0
    left_half = lax.broadcasted_iota(jnp.int32, (wide_rows, LANES), 1) < HALF

    def rate(m, level, kind):
        at = 4 * level + 2 * kind
        return jnp.concatenate(
            [rates_ref[m, at + c : at + c + 1, lane : lane + rows] for c in range(2)], 1
        )

    def make_turns(m, carry):
        tiles = []
        for level in range(levels):
            a, q = (jnp.broadcast_to(rate(m, level, kind), even.shape) for kind in range(2))
            base = jnp.where(even, a, q)
            first = base.astype(BF).astype(F32)
            rest = base - first
            second = rest.astype(BF).astype(F32)
            third = rest - second
            tile = jnp.where(row_id < 6, first, jnp.where(row_id < 10, second, third))
            tiles.append(jnp.where(row_id < 12, tile, jnp.where(row_id == 12, 1.0, 0.0)))
        turns_ref[m] = jnp.concatenate([*tiles, *tiles], 0).T.astype(BF)
        return carry

    lax.fori_loop(0, GROUP, make_turns, 0, unroll=2)

    def angles(firsts, seconds, thirds, stage):
        if not seconds:
            held = jnp.concatenate(firsts, 0)
        else:
            held = jnp.concatenate(
                [jnp.where(left_half, f, s) for f, s in zip(firsts, seconds)], 0
            )
        if not thirds:
            return jnp.dot(held, angle_ref[stage, :LANES], preferred_element_type=F32)
        held = jnp.concatenate([held, jnp.concatenate(thirds, 0)], 1)
        return jnp.dot(held, angle_ref[stage], preferred_element_type=F32)

    def combine(sources, turns, stage):
        phases = cos_turns(turns)
        highs, lows = [], []
        for n, pairs in enumerate(sources):
            high, low = [], []
            for s, (x, ix) in enumerate(pairs):
                phase = phases[n * wide_rows : (n + 1) * wide_rows, s * LANES : (s + 1) * LANES]
                turned = pltpu.roll(phase, HALF, 1)
                moved = x * jnp.where(left_half, phase, turned) + ix * jnp.where(left_half, turned, phase)
                top = moved.astype(BF)
                high.append(top)
                low.append((moved - top.astype(F32)).astype(BF))
            highs.append(jnp.concatenate(high, 1))
            lows.append(jnp.concatenate(low, 1))
        wide = jnp.dot(jnp.concatenate(highs, 0), mats_ref[stage], preferred_element_type=F32)
        narrow = jnp.dot(
            jnp.concatenate(lows, 0), mats_ref[stage, :, :LANES], preferred_element_type=F32
        )
        return wide[:, :LANES] + wide[:, LANES:] + narrow

    def times_i(x):
        other = pltpu.roll(x, HALF, 1)
        return jnp.where(left_half[: x.shape[0]], -other, other)

    def twice(x):
        return jnp.concatenate([x, x], 0)

    def level_stage(level, source, write):
        bit = levels - 1 - level

        def half_at(e):
            return pl.ds(pl.multiple_of(e * rows, rows), rows)

        def read(k, e):
            return source[k, half_at(e), :]

        def body(n, carry):
            sources, first, second, third, units = [], [], [], [], []
            for j in range(step):
                m = n * step + j
                e = (m >> (bit + 1)) & 1
                k1 = m | (2 << bit)
                k0 = k1 - (2 << bit)
                x0, x1 = read(k0, e), read(k1, e)
                sources.append(((twice(x0), twice(times_i(x0))), (twice(x1), twice(times_i(x1)))))
                if level:
                    second.append(twice(turns_ref[k0, half_at(e), :]))
                    third.append(twice(turns_ref[k1, half_at(e), :]))
                first.append(turns_ref[m])
                units.append(m)
            u = combine(sources, angles(first, second, third, level), level)
            for j, m in enumerate(units):
                write[m] = u[j * wide_rows : (j + 1) * wide_rows]
            return carry

        lax.fori_loop(0, GROUP // step, body, 0, unroll=UNROLL)

    level_stage(0, got_ref, state_a)
    level_stage(1, state_a, state_b)
    level_stage(2, state_b, state_a)
    level_stage(3, state_a, state_b)

    def last(n, carry):
        sources, first, second = [], [], []
        for j in range(step):
            i = n * step + j
            x0, x1 = state_b[2 * i], state_b[2 * i + 1]
            sources.append(((x0, times_i(x0)), (x1, times_i(x1))))
            first.append(turns_ref[2 * i])
            second.append(turns_ref[2 * i + 1])
        u = combine(sources, angles(first, second, [], levels), levels)
        for j in range(2 * step):
            out_ref[n * (2 * step) + j] = u[j * rows : (j + 1) * rows]
        return carry

    lax.fori_loop(0, GROUP // (2 * step), last, 0, unroll=UNROLL)


def finish(rows, step, got_ref, rates_ref, mats_ref, angle_ref, before_ref, out_ref, image, turns_ref, state_a, state_b, sems):
    ahead = before_ref.shape[1]
    held = pltpu.make_async_copy(before_ref, out_ref.at[:, pl.ds(0, ahead), :], sems.at[0])
    held.start()
    kernel(rows, ahead, step, got_ref, rates_ref, mats_ref, angle_ref, image, turns_ref, state_a, state_b)
    mine = pltpu.make_async_copy(image, out_ref.at[:, pl.ds(ahead, rows), :], sems.at[1])
    mine.start()
    mine.wait()
    held.wait()


def butterfly(got, rates, mats, angle, rows, step, before=None):
    whole = pl.BlockSpec(memory_space=pltpu.VMEM)
    in_specs = [whole] * 4
    scratch = [
        pltpu.VMEM((GROUP, 2 * rows, LANES), BF),
        pltpu.VMEM((GROUP, 2 * rows, LANES), F32),
        pltpu.VMEM((GROUP, 2 * rows, LANES), F32),
    ]
    cost = pl.CostEstimate(
        flops=GROUP * rows * 9 * 2 * 512 * 128, bytes_accessed=GROUP * rows * 9 * LANES * 4, transcendentals=0
    )
    params = pltpu.CompilerParams(vmem_limit_bytes=32 << 20)
    if before is None:
        return pl.pallas_call(
            functools.partial(kernel, rows, 0, step),
            out_shape=jax.ShapeDtypeStruct((GROUP, rows, LANES), F32),
            in_specs=in_specs,
            out_specs=whole,
            scratch_shapes=scratch,
            compiler_params=params,
            cost_estimate=cost,
        )(got, rates, mats, angle)
    return pl.pallas_call(
        functools.partial(finish, rows, step),
        out_shape=jax.ShapeDtypeStruct((GROUP, before.shape[1] + rows, LANES), F32),
        in_specs=[*in_specs, pl.BlockSpec(memory_space=pl.ANY)],
        out_specs=pl.BlockSpec(memory_space=pl.ANY),
        scratch_shapes=[pltpu.VMEM((GROUP, rows, LANES), F32), *scratch, pltpu.SemaphoreType.DMA((2,))],
        compiler_params=params,
        cost_estimate=cost,
    )(got, rates, mats, angle, before)


def stage_matrices(translate, evaluate):
    zero = jnp.zeros_like(translate)
    levels = jnp.concatenate(
        [jnp.concatenate([translate, zero], -1), jnp.concatenate([zero, translate], -1)], axis=2
    ).reshape(LEVELS, -1, LANES)
    er, ei = evaluate[:, 0], evaluate[:, 1]
    last = jnp.concatenate(
        [jnp.concatenate([er, ei], -1), jnp.concatenate([-ei, er], -1)], axis=1
    ).reshape(1, -1, LANES)
    whole = jnp.concatenate([levels, last], 0)
    high = lax.reduce_precision(whole, 8, 7)
    return jnp.concatenate([high, whole - high], -1).astype(BF)


def per_device(weights, rates, translate, evaluate):
    half = weights.shape[1] // 2
    axes = ("y", "zl", "band")
    other = lax.ppermute(evaluate[0], "band", [(0, 1), (1, 0)])
    mine = lax.axis_index("band")
    halves = weights[0].reshape(2, GROUP, SLICE, LANES)
    phase_rates = rates[0].reshape(16, GROUP, SLICE).transpose(1, 0, 2)

    def exchange(x):
        return lax.all_to_all(x, axes, 0, 0, tiled=True)

    block = jnp.concatenate([halves[0, :, :FIRST], halves[1, :, :FIRST], phase_rates], axis=1)
    block, other = lax.optimization_barrier((block, other))
    got = exchange(block)
    both = jnp.stack(
        [jnp.where(mine == 0, evaluate[0], other), jnp.where(mine == 0, other, evaluate[0])]
    )
    mats = stage_matrices(translate, both)
    angle = jnp.asarray(angle_matrix(LANES // 2))
    rest = jnp.concatenate([halves[0, :, FIRST:], halves[1, :, FIRST:]], axis=1)
    turns = got[:, 2 * FIRST :]
    rest, turns = lax.optimization_barrier((rest, turns))
    got_rest = exchange(rest)
    image = butterfly(got, turns, mats, angle, FIRST, STEPS[0])
    image = butterfly(got_rest, turns, mats, angle, SLICE - FIRST, STEPS[1], image)
    return exchange(image).reshape(half, LANES)


def solution(mesh):
    fine = Mesh(mesh.devices.reshape(4, 4, 4, 2, 2), ("y", "zl", "x", "core", "band"))
    leaf = ("y", "zl", "x", "core")
    return jax.shard_map(
        per_device,
        mesh=fine,
        in_specs=(P("band", leaf, None), P("band", None, None, leaf), P(), P("band", None, None, None)),
        out_specs=P((*leaf, "band"), None),
        check_vma=False,
    )
```

time: 249 us -> 213 us (0.86)
  waiting for transfers between devices: 99.7 us -> 74.7 us
  Pallas kernels: 65.2 us -> 43.3 us
  local copies, waits for them, and re-layouts: 5.29 us -> 11.2 us
  starting transfers between devices: 17.4 us -> 20.8 us
    ppermute x1, waiting for transfers between devices: 98 us -> 0.01 us  [per_device(): other = lax.ppermute(evaluate[0], 'band', [(0, 1), (1, 0)])]
    all_to_all x1 -> x2, waiting for transfers between devices: 1.69 us -> 74.7 us  [exchange(): return lax.all_to_all(x, axes, 0, 0, tiled=True)]
    pallas_call x1 -> x2, Pallas kernels: 65.2 us -> 43.3 us  [the longest x1 31.6 us: butterfly(): pl.pallas_call(functools.partial(kernel, rows, 0, step), out_shape=jax.Sh...]
    unnamed x7 -> x15, local copies, waits for them, and re-layouts: 1.33 us -> 5.76 us
    squeeze x0 -> x2, local copies, waits for them, and re-layouts: none -> 3.37 us  [the longest x1 2.09 us: per_device(): halves[0, :, :FIRST]]
    all_to_all x1 -> x2, starting transfers between devices: 11.7 us -> 13.6 us  [exchange(): return lax.all_to_all(x, axes, 0, 0, tiled=True)]
  transfers between devices with their start and end apart: 2 -> 3, of which waited for: 2 -> 1; matrix products, arithmetic and copies ran while one was open for 0% -> 4% of each run, Pallas kernels for 0% -> 15%
where the time goes in v2:
time: 213 us
  waiting for transfers between devices  74.7 us (35%)
  blocking collectives  59.2 us (28%)
  Pallas kernels  43.3 us (20%)
  starting transfers between devices  20.8 us (10%)
  local copies, waits for them, and re-layouts  11.2 us (5%)
  other arithmetic  3.46 us (2%)
    all_to_all x2, waiting for transfers between devices, exchange(): return lax.all_to_all(x, axes, 0, 0, tiled=True)  74.7 us
    all_to_all x1, blocking collectives, exchange(): return lax.all_to_all(x, axes, 0, 0, tiled=True)  59.2 us
    pallas_call x1, Pallas kernels, butterfly(): pl.pallas_call(functools.partial(kernel, rows, 0, step), out_shape=jax.Sh...  31.6 us
    all_to_all x2, starting transfers between devices, exchange(): return lax.all_to_all(x, axes, 0, 0, tiled=True)  13.6 us
    pallas_call x1, Pallas kernels, butterfly(): pl.pallas_call(functools.partial(finish, rows, step), out_shape=jax.Shape...  11.7 us
    ppermute x1, starting transfers between devices, per_device(): other = lax.ppermute(evaluate[0], 'band', [(0, 1), (1, 0)])  7.19 us
    unnamed x15, local copies, waits for them, and re-layouts  5.76 us
  transfers between devices with their start and end apart: 3, of which 1 were waited for; matrix products, arithmetic and copies ran while one was open for 4% of the time, Pallas kernels for 15%

profile of v2, /device:TPU:4, one launch (start us, length us, event | category | flops | bytes accessed | tf_op | source)
XLA Modules:
  0.0 212.9 jit_solution(15527815246317936819)
XLA Ops:
  0.0 7.2 %collective-permute-start = (f32[2,64,64]{2,1,0:T(8,128)}, f32[2,64,64]{2,1,0:T(8,128)S(1)}, u32[]{:S(2)}, u32[]{:S(2)}) collective-permute-start(f32[2,64,64]{2,1,0:T(8,128)} %bitcast.35), channel_id=1, source_target_pairs={{0,1},{1,0},{2,3},{3,2},{4,5},{5,4},{6,7},{7,6},{8,9},{9,8},{10,11... | collective-permute-start | bytes 98312 | tf_op jit(solution)/shard_map/ppermute | solution.py:276
  7.2 2.1 slice_bitcast_fusion.1
  9.3 1.2 reshape_squeeze.7
  10.5 0.2 copy.11
  10.6 1.9 pad_maximum_fusion
  12.6 8.2 %all-to-all-start = ((f32[32,208,128]{2,1,0:T(8,128)}), f32[32,208,128]{2,1,0:T(8,128)S(1)}, u32[]{:S(2)}, u32[]{:S(2)}) async-start(f32[32,208,128]{2,1,0:T(8,128)} %pad_maximum_fusion), calls=%async_computation | async-start | bytes 6815744 | tf_op jit(solution)/shard_map/all_to_all | solution.py:282
  20.8 1.3 slice_bitcast_fusion.3
  22.1 1.1 pad_maximum_fusion.1
  23.2 74.7 %all-to-all-done.got_ref = f32[32,208,128]{2,1,0:T(8,128)S(1)} async-done(((f32[32,208,128]{2,1,0:T(8,128)}), f32[32,208,128]{2,1,0:T(8,128)S(1)}, u32[]{:S(2)}, u32[]{:S(2)}) %all-to-all-start) | async-done | bytes 3407904 | tf_op jit(solution)/shard_map/all_to_all | solution.py:282
  97.9 0.7 slice.32.rates_ref
  98.6 1.7 copy-done
  100.3 5.4 %all-to-all-start.1 = ((f32[32,64,128]{2,1,0:T(8,128)}), f32[32,64,128]{2,1,0:T(8,128)S(1)}, u32[]{:S(2)}, u32[]{:S(2)}) async-start(f32[32,64,128]{2,1,0:T(8,128)} %pad_maximum_fusion.1), calls=%async_computation.1 | async-start | bytes 2097152 | tf_op jit(solution)/shard_map/all_to_all | solution.py:282
  105.8 0.1 select_maximum_fusion
  106.0 0.1 maximum_maximum_fusion
  106.1 0.1 reduce-precision_convert_fusion
  106.2 0.1 pad_maximum_fusion.3.mats_ref
  106.3 1.4 copy-done.1
  107.7 0.0 copy-done.2
  107.7 0.2 copy-done.3
  107.9 31.6 %shard_map.55.before_ref = f32[32,96,128]{2,1,0:T(8,128)S(1)} custom-call(f32[32,208,128]{2,1,0:T(8,128)S(1)} %copy-done.1, f32[32,16,128]{2,1,0:T(8,128)S(1)} %copy-done.2, bf16[5,256,256]{2,1,0:T(8,128)(2,1)S(1)} %pad_maximum_fusion.3.mats_ref, bf16[5,256,256]{2,1,0:T(8,128)(2,1)S(1)} %copy-done.3), custom_call_target="tpu_custom_call" | custom-call | flops 3623878656 | bytes 14155776 | tf_op jit(solution)/shard_map/pallas_call | solution.py:239
  139.6 1.1 copy-done.4
  140.7 11.7 %shard_map.56 = f32[32,128,128]{2,1,0:T(8,128)S(1)} custom-call(f32[32,64,128]{2,1,0:T(8,128)S(1)} %all-to-all-done.1.got_ref, f32[32,16,128]{2,1,0:T(8,128)S(1)} %copy-done.2, bf16[5,256,256]{2,1,0:T(8,128)(2,1)S(1)} %pad_maximum_fusion.3.mats_ref, bf16[5,256,256]{2,1,0:T(8,128)(2,1)S(1)} %copy-done.4, f32[32,96,128]{2,1,0:T(8,128)S(1)} %shard_map.55.before_ref), custom_call_target="tpu_custom_call" | custom-call | flops 1207959552 | bytes 4718592 | tf_op jit(solution)/shard_map/pallas_call | solution.py:248
  152.4 59.2 %all_to_all.15 = f32[32,128,128]{2,1,0:T(8,128)S(1)} all-to-all(f32[32,128,128]{2,1,0:T(8,128)S(1)} %shard_map.56), channel_id=1, replica_groups=mesh['y'=4,'zl'=4,'x'=4,'core'=2,'band'=2] {'y','zl','band'}, dimensions={0} | all-to-all | bytes 4194304 | tf_op jit(solution)/shard_map/all_to_all | solution.py:282
  211.5 1.3 copy.13
  (14 shorter events, 0.1 us)
Async XLA Ops:
  0.0 12.6 %collective-permute-start = (f32[2,64,64]{2,1,0:T(8,128)}, f32[2,64,64]{2,1,0:T(8,128)S(1)}, u32[]{:S(2)}, u32[]{:S(2)}) collective-permute-start(f32[2,64,64]{2,1,0:T(8,128)} %bitcast.35), channel_id=1, source_target_pairs={{0,1},{1,0},{2,3},{3,2},{4,5},{5,4},{6,7},{7,6},{8,9},{9,8},{10,11... | collective-permute-start | bytes 98312 | tf_op jit(solution)/shard_map/ppermute | solution.py:276
  12.6 85.3 %all-to-all-start = ((f32[32,208,128]{2,1,0:T(8,128)}), f32[32,208,128]{2,1,0:T(8,128)S(1)}, u32[]{:S(2)}, u32[]{:S(2)}) async-start(f32[32,208,128]{2,1,0:T(8,128)} %pad_maximum_fusion), calls=%async_computation | async-start | bytes 6815744 | tf_op jit(solution)/shard_map/all_to_all | solution.py:282
  23.2 82.7 %copy-start.6 = (f32[1,2,64,64]{3,2,1,0:T(8,128)S(1)}, f32[1,2,64,64]{3,2,1,0:T(8,128)}, u32[]{:S(2)}) copy-start(f32[1,2,64,64]{3,2,1,0:T(8,128)} %param.8) | copy-start | bytes 98308
  98.6 1.7 copy-start
  100.3 5.4 %copy-start.5 = (f32[4,2,64,64]{3,2,1,0:T(8,128)S(1)}, f32[4,2,64,64]{3,2,1,0:T(8,128)}, u32[]{:S(2)}) copy-start(f32[4,2,64,64]{3,2,1,0:T(8,128)} %param.7) | copy-start | bytes 393220
  100.3 39.2 %all-to-all-start.1 = ((f32[32,64,128]{2,1,0:T(8,128)}), f32[32,64,128]{2,1,0:T(8,128)S(1)}, u32[]{:S(2)}, u32[]{:S(2)}) async-start(f32[32,64,128]{2,1,0:T(8,128)} %pad_maximum_fusion.1), calls=%async_computation.1 | async-start | bytes 2097152 | tf_op jit(solution)/shard_map/all_to_all | solution.py:282
  105.7 2.0 copy-start.1
  105.7 2.0 copy-start.2
  105.7 2.2 %copy-start.3 = (bf16[5,256,256]{2,1,0:T(8,128)(2,1)S(1)}, bf16[5,256,256]{2,1,0:T(8,128)(2,1)}, u32[]{:S(2)}) copy-start(bf16[5,256,256]{2,1,0:T(8,128)(2,1)} %constant.10.clone.angle_ref) | copy-start | bytes 1966084
  139.6 1.1 copy-start.4

commit v3 on v2

--- a/solution.py
+++ b/solution.py
@@ -16,11 +16,13 @@
 TILE = 16
 MAGIC = 12582912.0
 LEVELS = 4
+FAR = pl.ANY
+PIECES = 8
 HALF = 64
 SLICE = 128
 FIRST = 96
 STEPS = (4, 16)
-UNROLL = 2
+UNROLL = 4
 
 
 def split3(values):
@@ -93,7 +95,7 @@
 C0, C1, C2, C3 = _fit()
 
 
-def kernel(rows, lane, step, got_ref, rates_ref, mats_ref, angle_ref, out_ref, turns_ref, state_a, state_b):
+def kernel(rows, lane, step, operands, rates_ref, mats_ref, angle_ref, out_ref, turns_ref, state_a, state_b):
     levels = LEVELS
     wide_rows = 2 * rows
     row_id = lax.broadcasted_iota(jnp.int32, (TILE, wide_rows), 0)
@@ -121,6 +123,8 @@
         return carry
 
     lax.fori_loop(0, GROUP, make_turns, 0, unroll=2)
+    for dma in operands:
+        dma.wait()
 
     def angles(firsts, seconds, thirds, stage):
         if not seconds:
@@ -189,9 +193,9 @@
                 write[m] = u[j * wide_rows : (j + 1) * wide_rows]
             return carry
 
-        lax.fori_loop(0, GROUP // step, body, 0, unroll=UNROLL)
-
-    level_stage(0, got_ref, state_a)
+        lax.fori_loop(0, GROUP // step, body, 0, unroll=min(UNROLL, GROUP // step))
+
+    level_stage(0, state_b, state_a)
     level_stage(1, state_a, state_b)
     level_stage(2, state_b, state_a)
     level_stage(3, state_a, state_b)
@@ -209,51 +213,105 @@
             out_ref[n * (2 * step) + j] = u[j * rows : (j + 1) * rows]
         return carry
 
-    lax.fori_loop(0, GROUP // (2 * step), last, 0, unroll=UNROLL)
-
-
-def finish(rows, step, got_ref, rates_ref, mats_ref, angle_ref, before_ref, out_ref, image, turns_ref, state_a, state_b, sems):
-    ahead = before_ref.shape[1]
-    held = pltpu.make_async_copy(before_ref, out_ref.at[:, pl.ds(0, ahead), :], sems.at[0])
-    held.start()
-    kernel(rows, ahead, step, got_ref, rates_ref, mats_ref, angle_ref, image, turns_ref, state_a, state_b)
-    mine = pltpu.make_async_copy(image, out_ref.at[:, pl.ds(ahead, rows), :], sems.at[1])
+    lax.fori_loop(0, GROUP // (2 * step), last, 0, unroll=min(UNROLL, max(1, GROUP // (2 * step))))
+
+
+def part(lane, rows, step, got_ref, first_ref, mats_far, angle_far, out_ref, image, rates, mats_ref, angle_ref, turns_ref, state_a, state_b, sems):
+    turns = pltpu.make_async_copy(first_ref.at[:, pl.ds(first_ref.shape[1] - 16, 16), :], rates, sems.at[0])
+    boxes = pltpu.make_async_copy(got_ref.at[:, pl.ds(0, 2 * rows), :], state_b, sems.at[1])
+    angle = pltpu.make_async_copy(angle_far, angle_ref, sems.at[2])
+    mats = pltpu.make_async_copy(mats_far, mats_ref, sems.at[3])
+    for dma in (turns, boxes, angle, mats):
+        dma.start()
+    turns.wait()
+    kernel(rows, lane, step, (boxes, angle, mats), rates, mats_ref, angle_ref, image, turns_ref, state_a, state_b)
+    mine = pltpu.make_async_copy(image, out_ref.at[:, pl.ds(lane, rows), :], sems.at[4])
     mine.start()
     mine.wait()
-    held.wait()
-
-
-def butterfly(got, rates, mats, angle, rows, step, before=None):
-    whole = pl.BlockSpec(memory_space=pltpu.VMEM)
-    in_specs = [whole] * 4
-    scratch = [
-        pltpu.VMEM((GROUP, 2 * rows, LANES), BF),
-        pltpu.VMEM((GROUP, 2 * rows, LANES), F32),
-        pltpu.VMEM((GROUP, 2 * rows, LANES), F32),
-    ]
-    cost = pl.CostEstimate(
-        flops=GROUP * rows * 9 * 2 * 512 * 128, bytes_accessed=GROUP * rows * 9 * LANES * 4, transcendentals=0
-    )
-    params = pltpu.CompilerParams(vmem_limit_bytes=32 << 20)
-    if before is None:
-        return pl.pallas_call(
-            functools.partial(kernel, rows, 0, step),
-            out_shape=jax.ShapeDtypeStruct((GROUP, rows, LANES), F32),
-            in_specs=in_specs,
-            out_specs=whole,
-            scratch_shapes=scratch,
-            compiler_params=params,
-            cost_estimate=cost,
-        )(got, rates, mats, angle)
+
+
+def begin(rows, step, got_ref, mats_far, angle_far, out_ref, *scratch):
+    part(0, rows, step, got_ref, got_ref, mats_far, angle_far, out_ref, *scratch)
+
+
+def finish(lane, rows, step, got_ref, first_ref, mats_far, angle_far, before_ref, out_ref, *scratch):
+    part(lane, rows, step, got_ref, first_ref, mats_far, angle_far, out_ref, *scratch)
+
+
+def fill_message(rows, weights_ref, rates_ref, out_ref, held, sems):
+    share = GROUP // PIECES
+    arrive, leave = [], []
+    for n in range(PIECES):
+        at = pl.ds(n * share, share)
+        for e in range(2):
+            into = held.at[at, pl.ds(e * rows, rows), :]
+            arrive.append(
+                pltpu.make_async_copy(weights_ref.at[e, at, pl.ds(0, rows), :], into, sems.at[0, 2 * n + e])
+            )
+        leave.append(pltpu.make_async_copy(held.at[at], out_ref.at[at], sems.at[1, n]))
+    for dma in arrive:
+        dma.start()
+    half = GROUP * LANES
+
+    def move(p, carry):
+        for level in range(LEVELS):
+            for child in range(2):
+                at = pl.ds(pl.multiple_of(child * half + p * LANES, LANES), LANES)
+                for kind in range(2):
+                    row = 2 * rows + 4 * level + 2 * kind + child
+                    held[p, row : row + 1, :] = rates_ref[level, kind : kind + 1, at]
+        return carry
+
+    lax.fori_loop(0, GROUP, move, 0, unroll=4)
+    for n in range(PIECES):
+        arrive[2 * n].wait()
+        arrive[2 * n + 1].wait()
+        leave[n].start()
+    for dma in leave:
+        dma.wait()
+
+
+def first_message(halves, rates):
     return pl.pallas_call(
-        functools.partial(finish, rows, step),
-        out_shape=jax.ShapeDtypeStruct((GROUP, before.shape[1] + rows, LANES), F32),
-        in_specs=[*in_specs, pl.BlockSpec(memory_space=pl.ANY)],
-        out_specs=pl.BlockSpec(memory_space=pl.ANY),
-        scratch_shapes=[pltpu.VMEM((GROUP, rows, LANES), F32), *scratch, pltpu.SemaphoreType.DMA((2,))],
-        compiler_params=params,
-        cost_estimate=cost,
-    )(got, rates, mats, angle, before)
+        functools.partial(fill_message, FIRST),
+        out_shape=jax.ShapeDtypeStruct((GROUP, 2 * FIRST + 16, LANES), F32),
+        in_specs=[pl.BlockSpec(memory_space=FAR), pl.BlockSpec(memory_space=pltpu.VMEM)],
+        out_specs=pl.BlockSpec(memory_space=FAR),
+        scratch_shapes=[
+            pltpu.VMEM((GROUP, 2 * FIRST + 16, LANES), F32),
+            pltpu.SemaphoreType.DMA((2, 2 * PIECES)),
+        ],
+        cost_estimate=pl.CostEstimate(flops=0, bytes_accessed=8 << 20, transcendentals=0),
+    )(halves, rates)
+
+
+def butterfly(got, mats, angle, rows, step, first=None, before=None):
+    far = pl.BlockSpec(memory_space=FAR)
+    operands = [got, mats, angle] if before is None else [got, first, mats, angle, before]
+    body = begin if before is None else functools.partial(finish, SLICE - rows)
+    return pl.pallas_call(
+        functools.partial(body, rows, step),
+        out_shape=jax.ShapeDtypeStruct((GROUP, SLICE, LANES), F32),
+        in_specs=[far] * len(operands),
+        out_specs=far,
+        scratch_shapes=[
+            pltpu.VMEM((GROUP, rows, LANES), F32),
+            pltpu.VMEM((GROUP, 16, LANES), F32),
+            pltpu.VMEM(mats.shape, BF),
+            pltpu.VMEM(angle.shape, BF),
+            pltpu.VMEM((GROUP, 2 * rows, LANES), BF),
+            pltpu.VMEM((GROUP, 2 * rows, LANES), F32),
+            pltpu.VMEM((GROUP, 2 * rows, LANES), F32),
+            pltpu.SemaphoreType.DMA((5,)),
+        ],
+        input_output_aliases={} if before is None else {4: 0},
+        compiler_params=pltpu.CompilerParams(vmem_limit_bytes=60 << 20),
+        cost_estimate=pl.CostEstimate(
+            flops=GROUP * rows * 9 * 2 * 512 * 128,
+            bytes_accessed=GROUP * rows * 9 * LANES * 4,
+            transcendentals=0,
+        ),
+    )(*operands)
 
 
 def stage_matrices(translate, evaluate):
@@ -276,13 +334,11 @@
     other = lax.ppermute(evaluate[0], "band", [(0, 1), (1, 0)])
     mine = lax.axis_index("band")
     halves = weights[0].reshape(2, GROUP, SLICE, LANES)
-    phase_rates = rates[0].reshape(16, GROUP, SLICE).transpose(1, 0, 2)
 
     def exchange(x):
         return lax.all_to_all(x, axes, 0, 0, tiled=True)
 
-    block = jnp.concatenate([halves[0, :, :FIRST], halves[1, :, :FIRST], phase_rates], axis=1)
-    block, other = lax.optimization_barrier((block, other))
+    block, other = lax.optimization_barrier((first_message(halves, rates[0]), other))
     got = exchange(block)
     both = jnp.stack(
         [jnp.where(mine == 0, evaluate[0], other), jnp.where(mine == 0, other, evaluate[0])]
@@ -290,11 +346,10 @@
     mats = stage_matrices(translate, both)
     angle = jnp.asarray(angle_matrix(LANES // 2))
     rest = jnp.concatenate([halves[0, :, FIRST:], halves[1, :, FIRST:]], axis=1)
-    turns = got[:, 2 * FIRST :]
-    rest, turns = lax.optimization_barrier((rest, turns))
+    rest, mats = lax.optimization_barrier((rest, mats))
     got_rest = exchange(rest)
-    image = butterfly(got, turns, mats, angle, FIRST, STEPS[0])
-    image = butterfly(got_rest, turns, mats, angle, SLICE - FIRST, STEPS[1], image)
+    image = butterfly(got, mats, angle, FIRST, STEPS[0])
+    image = butterfly(got_rest, mats, angle, SLICE - FIRST, STEPS[1], got, image)
     return exchange(image).reshape(half, LANES)
 
 

time: 213 us -> 210 us (0.986)
  local copies, waits for them, and re-layouts: 11.2 us -> 2.64 us
  Pallas kernels: 43.3 us -> 49.9 us
  waiting for transfers between devices: 74.7 us -> 72.3 us
    pallas_call x2 -> x3, Pallas kernels: 43.3 us -> 49.9 us  [the longest x2 45.9 us: butterfly(): pl.pallas_call(functools.partial(body, rows, step), out_shape=jax.ShapeDt...]
    unnamed x15 -> x5, local copies, waits for them, and re-layouts: 5.76 us -> 1.33 us
    all_to_all x2, waiting for transfers between devices: 74.7 us -> 72.3 us  [exchange(): return lax.all_to_all(x, axes, 0, 0, tiled=True)]
  transfers between devices with their start and end apart: 3 -> 3, of which waited for: 1 -> 1; matrix products, arithmetic and copies ran while one was open for 4% -> 2% of each run, Pallas kernels for 15% -> 17%
where the time goes in v3:
time: 210 us
  waiting for transfers between devices  72.3 us (34%)
  blocking collectives  59.3 us (28%)
  Pallas kernels  49.9 us (24%)
  starting transfers between devices  22.1 us (11%)
  other arithmetic  3.39 us (2%)
  local copies, waits for them, and re-layouts  2.64 us (1%)
    all_to_all x2, waiting for transfers between devices, exchange(): return lax.all_to_all(x, axes, 0, 0, tiled=True)  72.3 us
    all_to_all x1, blocking collectives, exchange(): return lax.all_to_all(x, axes, 0, 0, tiled=True)  59.3 us
    pallas_call x2, Pallas kernels, butterfly(): pl.pallas_call(functools.partial(body, rows, step), out_shape=jax.ShapeDt...  45.9 us
    all_to_all x2, starting transfers between devices, exchange(): return lax.all_to_all(x, axes, 0, 0, tiled=True)  14.9 us
    ppermute x1, starting transfers between devices, per_device(): other = lax.ppermute(evaluate[0], 'band', [(0, 1), (1, 0)])  7.19 us
  transfers between devices with their start and end apart: 3, of which 1 were waited for; matrix products, arithmetic and copies ran while one was open for 2% of the time, Pallas kernels for 17%

profile of v3, /device:TPU:4, one launch (start us, length us, event | category | flops | bytes accessed | tf_op | source)
XLA Modules:
  0.0 209.8 jit_solution(10030850805847953186)
XLA Ops:
  0.0 7.2 %collective-permute-start = (f32[2,64,64]{2,1,0:T(8,128)}, f32[2,64,64]{2,1,0:T(8,128)S(1)}, u32[]{:S(2)}, u32[]{:S(2)}) collective-permute-start(f32[2,64,64]{2,1,0:T(8,128)} %bitcast.29), channel_id=1, source_target_pairs={{0,1},{1,0},{2,3},{3,2},{4,5},{5,4},{6,7},{7,6},{8,9},{9,8},{10,11... | collective-permute-start | bytes 98312 | tf_op jit(solution)/shard_map/ppermute | solution.py:334
  7.2 4.0 %shard_map.55 = f32[32,208,128]{2,1,0:T(8,128)} custom-call(f32[2,32,128,128]{3,2,1,0:T(8,128)} %bitcast.24, f32[4,2,8192]{2,1,0:T(2,128)} %bitcast.28), custom_call_target="tpu_custom_call" | custom-call | bytes 8388608 | tf_op jit(solution)/shard_map/pallas_call | solution.py:275
  11.2 0.0 collective-permute-done
  11.2 9.6 %all-to-all-start.1 = ((f32[32,208,128]{2,1,0:T(8,128)}), f32[32,208,128]{2,1,0:T(8,128)S(1)}, u32[]{:S(2)}, u32[]{:S(2)}) async-start(f32[32,208,128]{2,1,0:T(8,128)} %shard_map.55), calls=%async_computation.1 | async-start | bytes 6815744 | tf_op jit(solution)/shard_map/all_to_all | solution.py:339
  20.8 1.2 select_maximum_fusion
  22.0 0.0 copy-start.1
  22.0 1.3 slice_bitcast_fusion.1
  23.3 1.1 pad_maximum_fusion
  24.4 0.0 copy-done.1
  24.4 0.1 maximum_maximum_fusion
  24.5 0.1 reduce-precision_convert_fusion
  24.7 0.9 pad_maximum_fusion.2.mats_far
  25.6 72.3 %all-to-all-done.1.got_ref.first_ref = f32[32,208,128]{2,1,0:T(8,128)S(1)} async-done(((f32[32,208,128]{2,1,0:T(8,128)}), f32[32,208,128]{2,1,0:T(8,128)S(1)}, u32[]{:S(2)}, u32[]{:S(2)}) %all-to-all-start.1) | async-done | bytes 3407904 | tf_op jit(solution)/shard_map/all_to_all | solution.py:339
  97.9 0.0 copy-start
  97.9 5.4 %all-to-all-start = ((f32[32,64,128]{2,1,0:T(8,128)}), f32[32,64,128]{2,1,0:T(8,128)}, u32[]{:S(2)}, u32[]{:S(2)}) async-start(f32[32,64,128]{2,1,0:T(8,128)} %pad_maximum_fusion), calls=%async_computation | async-start | bytes 2097152 | tf_op jit(solution)/shard_map/all_to_all | solution.py:339
  103.3 0.0 copy-done
  103.3 32.5 %shard_map.56.before_ref = f32[32,128,128]{2,1,0:T(8,128)} custom-call(f32[32,208,128]{2,1,0:T(8,128)} %copy-done, bf16[5,256,256]{2,1,0:T(8,128)(2,1)} %pad_maximum_fusion.2.mats_far, bf16[5,256,256]{2,1,0:T(8,128)(2,1)} %constant.10.clone.angle_far), custom_call_target="tpu_custom_call" | custom-call | flops 3623878656 | bytes 14155776 | tf_op jit(solution)/shard_map/pallas_call | solution.py:292
  135.8 0.0 all-to-all-done.got_ref
  135.9 13.3 %shard_map.57 = f32[32,128,128]{2,1,0:T(8,128)} custom-call(f32[32,64,128]{2,1,0:T(8,128)} %all-to-all-done.got_ref, f32[32,208,128]{2,1,0:T(8,128)} %copy-done, bf16[5,256,256]{2,1,0:T(8,128)(2,1)} %pad_maximum_fusion.2.mats_far, bf16[5,256,256]{2,1,0:T(8,128)(2,1)} %constant.10.clone.angle_far, ...), custom_call_target="tpu_custom_call", output_to_operand_aliasing={{}: (4, {})} | custom-call | flops 1207959552 | bytes 4718592 | tf_op jit(solution)/shard_map/pallas_call | solution.py:292
  149.2 59.3 %all_to_all.15 = f32[32,128,128]{2,1,0:T(8,128)S(1)} all-to-all(f32[32,128,128]{2,1,0:T(8,128)} %shard_map.57), channel_id=1, replica_groups=mesh['y'=4,'zl'=4,'x'=4,'core'=2,'band'=2] {'y','zl','band'}, dimensions={0} | all-to-all | bytes 4194304 | tf_op jit(solution)/shard_map/all_to_all | solution.py:339
  208.5 1.3 copy.11
  (3 shorter events, 0.0 us)
Async XLA Ops:
  0.0 11.2 %collective-permute-start = (f32[2,64,64]{2,1,0:T(8,128)}, f32[2,64,64]{2,1,0:T(8,128)S(1)}, u32[]{:S(2)}, u32[]{:S(2)}) collective-permute-start(f32[2,64,64]{2,1,0:T(8,128)} %bitcast.29), channel_id=1, source_target_pairs={{0,1},{1,0},{2,3},{3,2},{4,5},{5,4},{6,7},{7,6},{8,9},{9,8},{10,11... | collective-permute-start | bytes 98312 | tf_op jit(solution)/shard_map/ppermute | solution.py:334
  11.2 86.7 %all-to-all-start.1 = ((f32[32,208,128]{2,1,0:T(8,128)}), f32[32,208,128]{2,1,0:T(8,128)S(1)}, u32[]{:S(2)}, u32[]{:S(2)}) async-start(f32[32,208,128]{2,1,0:T(8,128)} %shard_map.55), calls=%async_computation.1 | async-start | bytes 6815744 | tf_op jit(solution)/shard_map/all_to_all | solution.py:339
  22.0 2.4 %copy-start.1 = (f32[1,2,64,64]{3,2,1,0:T(8,128)S(1)}, f32[1,2,64,64]{3,2,1,0:T(8,128)}, u32[]{:S(2)}) copy-start(f32[1,2,64,64]{3,2,1,0:T(8,128)} %param.8) | copy-start | bytes 98308
  97.9 5.4 %copy-start = (f32[32,208,128]{2,1,0:T(8,128)}, f32[32,208,128]{2,1,0:T(8,128)S(1)}, u32[]{:S(2)}) copy-start(f32[32,208,128]{2,1,0:T(8,128)S(1)} %all-to-all-done.1.got_ref.first_ref) | copy-start | bytes 10223620
  97.9 37.9 %all-to-all-start = ((f32[32,64,128]{2,1,0:T(8,128)}), f32[32,64,128]{2,1,0:T(8,128)}, u32[]{:S(2)}, u32[]{:S(2)}) async-start(f32[32,64,128]{2,1,0:T(8,128)} %pad_maximum_fusion), calls=%async_computation | async-start | bytes 2097152 | tf_op jit(solution)/shard_map/all_to_all | solution.py:339
